TPU v7x, 256 devices: a whole 4x4x8 slice. The times are simulated.
256 devices in a mesh: ctx: 32 (over y, z), exp: 8 (over x, core).
Axes of the slice: x: 4, y: 4, z: 8, core: 2. Of those that a mesh axis runs over, the one named last changes fastest.
Arguments:
- query_rows: bfloat16 [8, 4096, 4096], P('exp', 'ctx'), may hold values from -150 to 150, as said below
- key_matrix_all: bfloat16 [8, 4096, 512], P('exp', 'ctx'), may hold values from -5 to 5
- value_matrix_all: bfloat16 [8, 4096, 512], P('exp', 'ctx'), may hold values from -6 to 6
- context_grad: bfloat16 [8, 4096, 4096], P('exp', 'ctx'), may hold values from -6 to 6
- mixture_input: bfloat16 [8, 4096, 2048], P('exp', 'ctx'), may hold values from -6 to 6
- mixture_grad: bfloat16 [8, 4096, 2048], P('exp', 'ctx'), may hold values from -6 to 6
- expert_ids: int32 [8, 4096, 8], P('exp', 'ctx'), may hold values from 0 to 127, as said below
- route_weight: bfloat16 [8, 4096, 8], P('exp', 'ctx'), may hold values from 0.049804688 to 0.5
- gate_weight: bfloat16 [8, 2048, 768], P('exp', 'ctx'), may hold values from -0.125 to 0.125
- up_weight: bfloat16 [8, 2048, 768], P('exp', 'ctx'), may hold values from -0.125 to 0.125
- down_weight: bfloat16 [8, 2048, 768], P('exp', 'ctx'), may hold values from -0.21875 to 0.21875
Outputs:
- query_grad: bfloat16 [8, 4096, 4096], P('exp', 'ctx')
- key_grad: bfloat16 [8, 4096, 512], P('exp', 'ctx')
- value_grad: bfloat16 [8, 4096, 512], P('exp', 'ctx')
- input_grad: bfloat16 [8, 4096, 2048], P('exp', 'ctx')
- route_grad: bfloat16 [8, 4096, 8], P('exp', 'ctx')
- gate_grad: bfloat16 [8, 2048, 768], P('exp', 'ctx')
- up_grad: bfloat16 [8, 2048, 768], P('exp', 'ctx')
- down_grad: bfloat16 [8, 2048, 768], P('exp', 'ctx')
Inputs may be any that keep to these rules, and one draw needn't show every extreme that they name: query_rows and key_matrix_all may have rows aligned with each other. `expert_ids`: each token names 8 different experts. Among the 128 tokens of one device at most 8 name any one expert of the window, and in every draw one expert of the window is named by exactly 8 tokens of every device.
All inputs are finite; a program needn't handle non-finite values.
Results may differ from a plain program's by a relative error of at most 0.025.
Values may be sent and summed in bfloat16 or wider, within the bound.
A program may use at most 192 MiB of HBM per device.

v0:
```python
import math

import jax
import jax.numpy as jnp
from jax import lax
from jax.experimental import pallas as pl
from jax.experimental.pallas import tpu as pltpu
from jax.sharding import PartitionSpec as P

D = 2048
QUERY_HEADS = 32
KEY_VALUE_HEADS = 4
HEAD_SIZE = 128
FF = 768
EXPERTS = 128
TOPK = 8
CAP = 8
NY = 4
NZ = 8
NE = 8
TOK = 128
GW = QUERY_HEADS // KEY_VALUE_HEADS * HEAD_SIZE
DS = D // NY
WD = D // (NY * NZ)
KC = 512
HALF = 4
ROWS = HALF * TOK
STEPS = NY * (GW // (HALF * HEAD_SIZE))
MESH = pl.DeviceIdType.MESH
VMEM_MOST = 60 * 1024 * 1024
BF = jnp.bfloat16
F32 = jnp.float32


def places():
    ctx = lax.axis_index("ctx")
    return lax.div(ctx, NZ), lax.rem(ctx, NZ), lax.axis_index("exp")


def at_y(y, z, e, shift):
    peer = lax.rem(y + shift, NY)
    return peer, (peer * NZ + z, e)


def at_z(y, z, e, shift):
    peer = lax.rem(z + shift + NZ, NZ)
    return peer, (y * NZ + peer, e)


def at_e(y, z, e, shift):
    peer = lax.rem(e + shift, NE)
    return peer, (y * NZ + z, peer)


def greet(peers):
    barrier = pltpu.get_barrier_semaphore()
    for peer in peers:
        pl.semaphore_signal(barrier, inc=1, device_id=peer, device_id_type=MESH)
    pl.semaphore_wait(barrier, len(peers))


def remote(src, dst, send, recv, index, peer):
    return pltpu.make_async_remote_copy(
        src_ref=src,
        dst_ref=dst,
        send_sem=send.at[index],
        recv_sem=recv.at[index],
        device_id=peer,
        device_id_type=MESH,
    )


def columns(index, width):
    return pl.ds(pl.multiple_of(index * width, width), width)


def dot(a, b, left, right):
    return lax.dot_general(a, b, (((left,), (right,)), ((), ())), preferred_element_type=F32)


def layer_kernel(
    q, do, k, v, wg, wu, wd, x_in, c_in, ids, route_weight,
    dq_home, dk_home, dv_home, gg_out, gu_out, gd_out, input_grad, route_grad,
    rows, dispatch, route_home,
    q_all, do_all, k_all, v_all, kt, q_st, do_st, s_scr, g_scr, dk_acc, dv_acc, dqt, dq,
    rows_own, xc, x_t, c_t, wg_all, wu_all, wd_all, part, parts, act, route,
    rb, rbuf, back, gg, gu, gd,
    kv_right, kv_left, g_right, g_left, u_right, u_left, d_right, d_left, kv_first, kv_sum,
    local_sem, y_send, y_recv, e_send, e_recv, x_send, x_recv, r_send, r_recv, l_send, l_recv,
    s_send, s_recv, a_send, a_recv, t_send, t_recv, q_send, q_recv, b_send, b_recv,
    i_send, i_recv, h_send, h_recv, gr_send, gr_recv, gl_send, gl_recv,
):
    y, z, e = places()
    count = NY * NE * CAP
    scale = 1.0 / math.sqrt(HEAD_SIZE)
    factor = scale * math.log2(math.e)
    greet(
        [at_y(y, z, e, d)[1] for d in range(1, NY)]
        + [at_z(y, z, e, d)[1] for d in (1, -1)]
        + [at_e(y, z, e, d)[1] for d in range(1, NE)]
    )
    right = at_z(y, z, e, 1)[1]
    left = at_z(y, z, e, -1)[1]

    def tokens():
        return [
            remote(rows.at[at_e(y, z, e, d)[0]], rows_own.at[e], e_send, e_recv, d - 1,
                   at_e(y, z, e, d)[1])
            for d in range(1, NE)
        ]

    def slices():
        return [
            remote(rows_own.at[:, :, columns(at_y(y, z, e, d)[0], DS)], xc.at[y], x_send, x_recv,
                   d - 1, at_y(y, z, e, d)[1])
            for d in range(1, NY)
        ]

    def y_exchange(src, target, width, base):
        return [
            remote(src.at[:, columns(at_y(y, z, e, d)[0], width)], target, y_send, y_recv,
                   base + d - 1, at_y(y, z, e, d)[1])
            for d in range(1, NY)
        ]

    def kv_exchange():
        return y_exchange(k, k_all.at[y, z], HEAD_SIZE, 0) + y_exchange(
            v, v_all.at[y, z], HEAD_SIZE, 3
        )

    def q_exchange():
        return y_exchange(q, q_all.at[y], GW, 6) + y_exchange(do, do_all.at[y], GW, 9)

    gathered = (
        lambda b: wg_all.at[b],
        lambda b: wu_all.at[b],
        lambda b: wd_all.at[b],
        lambda b: k_all.at[:, b],
        lambda b: v_all.at[:, b],
    )

    def gather(index, step):
        block = gathered[index]
        here = block(lax.rem(z - step + NZ, NZ))
        pair = [remote(here, here, r_send, r_recv, index * 4 + step, right)]
        if step < 3:
            there = block(lax.rem(z + step, NZ))
            pair.append(remote(there, there, l_send, l_recv, index * 3 + step, left))
        return pair

    def gather_step(indices, step):
        for index in indices:
            if step > 0:
                for c in gather(index, step - 1):
                    c.wait_recv()
            if step < 4:
                for c in gather(index, step):
                    c.start()

    def here(src, dst, index):
        return pltpu.make_async_copy(src, dst, local_sem.at[index])

    for c in kv_exchange():
        c.start()
    own = [
        here(k.at[:, columns(y, HEAD_SIZE)], k_all.at[y, z], 1),
        here(v.at[:, columns(y, HEAD_SIZE)], v_all.at[y, z], 2),
        here(q.at[:, columns(y, GW)], q_all.at[y], 3),
        here(do.at[:, columns(y, GW)], do_all.at[y], 4),
        here(wg, wg_all.at[z], 5),
        here(wu, wu_all.at[z], 6),
        here(wd, wd_all.at[z], 7),
    ]
    for c in own:
        c.start()
    for c in own[4:]:
        c.wait()
    gather_step((0, 1, 2), 0)

    slot = lax.broadcasted_iota(jnp.int32, (NE * CAP, TOK), 0)
    expert = lax.div(slot, CAP) * (EXPERTS // NE)

    def named(j):
        return (ids[j : j + 1, :] == expert).astype(F32)

    combine = route_weight[...].astype(F32)
    taken = jnp.zeros((NE * CAP, TOK), F32)
    weights = jnp.zeros((NE * CAP, TOK), F32)
    for j in range(TOPK):
        hit = named(j)
        taken += hit
        weights += hit * combine[j : j + 1, :]
    earlier = (
        lax.broadcasted_iota(jnp.int32, (TOK, TOK), 0)
        < lax.broadcasted_iota(jnp.int32, (TOK, TOK), 1)
    ).astype(F32)
    place = dot(taken.astype(BF), earlier.astype(BF), 1, 0)
    placed = taken * (place == lax.rem(slot, CAP).astype(F32)).astype(F32)
    dispatch[...] = placed.T.astype(BF)
    collect = placed.astype(BF)
    rows[:, :, :D] = jnp.concatenate(
        [dot(collect, r[...], 1, 0).reshape(NE, CAP, D) for r in (x_in, c_in)], axis=1
    ).astype(BF)
    weight_col = jnp.sum(placed * weights, axis=1, keepdims=True)
    weight_col = jnp.broadcast_to(weight_col, (NE * CAP, 128)).reshape(NE, CAP, 128)
    rows[:, :, D:] = jnp.concatenate([weight_col, weight_col], axis=1).astype(BF)
    for c in tokens():
        c.start()
    own_rows = here(rows.at[e], rows_own.at[e], 0)
    own_rows.start()

    for c in kv_exchange():
        c.wait_recv()
    for c in own[:4]:
        c.wait()
    gather_step((3, 4), 0)
    for c in q_exchange():
        c.start()
    for c in tokens():
        c.wait_recv()
    own_rows.wait()
    for c in slices():
        c.start()
    own_xc = here(rows_own.at[:, :, columns(y, DS)], xc.at[y], 8)
    own_xc.start()
    dk_acc[...] = jnp.zeros_like(dk_acc)
    dv_acc[...] = jnp.zeros_like(dv_acc)
    for step in range(1, 4):
        gather_step((3, 4), step)
    gather_step((0, 1, 2), 1)
    own_xc.wait()
    for c in slices():
        c.wait_recv()
    both = xc[...].astype(F32)
    x_t[...] = both[:, :, :CAP, :].reshape(count, DS).T.astype(BF)
    c_t[...] = both[:, :, CAP:, :].reshape(count, DS).T.astype(BF)
    gather_step((3, 4), 4)
    for c in q_exchange():
        c.wait_recv()

    def chunk(c):
        per = NZ * TOK // KC
        return lax.div(c, per), pl.ds(lax.rem(c, per) * (KC // TOK), KC // TOK)

    def chunk_rows(ref, c):
        a, b = chunk(c)
        return ref[a, b].reshape(KC, HEAD_SIZE)

    def at(c):
        return pl.ds(pl.multiple_of(c * KC, KC), KC)

    def turn(c, carry):
        kt[:, at(c)] = chunk_rows(k_all, c).astype(F32).T.astype(BF)
        return carry

    lax.fori_loop(0, NY * NZ * TOK // KC, turn, 0)

    def fold(values, op):
        return op(values.reshape(KC // 8, 8, ROWS), axis=0)

    def attend(block, half, event):
        position = block * NZ + z
        chunks = lax.div(position * TOK + TOK + KC - 1, KC)
        for h in range(HALF):
            cols = pl.ds(
                pl.multiple_of(half * (HALF * HEAD_SIZE) + h * HEAD_SIZE, HEAD_SIZE), HEAD_SIZE
            )
            q_st[h * TOK : (h + 1) * TOK, :] = q_all[block, :, cols]
            do_st[h * TOK : (h + 1) * TOK, :] = do_all[block, :, cols]

        def scores(c, peak, masked):
            s = dot(chunk_rows(k_all, c), q_st[...], 1, 1) * factor
            if masked:
                key_pos = c * KC + lax.broadcasted_iota(jnp.int32, (KC, ROWS), 0)
                query_pos = position * TOK + lax.rem(
                    lax.broadcasted_iota(jnp.int32, (KC, ROWS), 1), TOK
                )
                s = jnp.where(key_pos <= query_pos, s, -1e30)
            s_scr[at(c), :] = s
            return jnp.maximum(peak, fold(s, jnp.max))

        peak = lax.fori_loop(
            0, chunks - 1, lambda c, m: scores(c, m, False), jnp.full((8, ROWS), -1e30, F32)
        )
        peak = scores(chunks - 1, peak, True)
        peak = jnp.max(peak, axis=0, keepdims=True)
        event(0)

        def weigh(c, carry):
            total, paired = carry
            p = jnp.exp2(s_scr[at(c), :] - peak)
            g = dot(chunk_rows(v_all, c), do_st[...], 1, 1)
            s_scr[at(c), :] = p
            g_scr[at(c), :] = g
            return total + fold(p, jnp.sum), paired + fold(p * g, jnp.sum)

        zero = jnp.zeros((8, ROWS), F32)
        total, paired = lax.fori_loop(0, chunks, weigh, (zero, zero))
        inverse = 1.0 / jnp.sum(total, axis=0, keepdims=True)
        row_dot = jnp.sum(paired, axis=0, keepdims=True) * inverse
        event(1)

        dqt[...] = jnp.zeros_like(dqt)

        def gradients(c, carry):
            a, b = chunk(c)
            p = s_scr[at(c), :] * inverse
            ds = (p * (g_scr[at(c), :] - row_dot)).astype(BF)
            shape = (KC // TOK, TOK, HEAD_SIZE)
            dv_acc[a, b] += dot(p.astype(BF), do_st[...], 1, 0).reshape(shape)
            dk_acc[a, b] += dot(ds, q_st[...], 1, 0).reshape(shape)
            dqt[...] += dot(kt[:, at(c)], ds, 1, 0)
            return carry

        lax.fori_loop(0, chunks, gradients, 0)
        for h in range(HALF):
            cols = pl.ds(
                pl.multiple_of(half * (HALF * HEAD_SIZE) + h * HEAD_SIZE, HEAD_SIZE), HEAD_SIZE
            )
            dq[block, :, cols] = (dqt[:, h * TOK : (h + 1) * TOK] * scale).T.astype(BF)
        event(2)

    def swaps():
        return [
            remote(part.at[at_y(y, z, e, d)[0]], parts.at[d - 1], s_send, s_recv, d - 1,
                   at_y(y, z, e, d)[1])
            for d in range(1, NY)
        ]

    def spreads():
        return [
            remote(act.at[y], act.at[y], a_send, a_recv, d - 1, at_y(y, z, e, d)[1])
            for d in range(1, NY)
        ]

    def routes():
        return [
            remote(route.at[at_e(y, z, e, d)[0]], route_home.at[e], t_send, t_recv, d - 1,
                   at_e(y, z, e, d)[1])
            for d in range(1, NE)
        ]

    def row_swaps():
        return [
            remote(rb.at[at_y(y, z, e, d)[0]], rbuf.at[y], b_send, b_recv, d - 1,
                   at_y(y, z, e, d)[1])
            for d in range(1, NY)
        ]

    def quarter(block):
        def value(b):
            return jnp.stack([dk_acc[block, b] * scale, dv_acc[block, b]])

        return value

    summed = [
        (lambda b: gg[b].astype(F32), lambda t: g_right.at[t], lambda t: g_left.at[t], gg_out),
        (lambda b: gu[b].astype(F32), lambda t: u_right.at[t], lambda t: u_left.at[t], gu_out),
        (lambda b: gd[b].astype(F32), lambda t: d_right.at[t], lambda t: d_left.at[t], gd_out),
    ]
    for block in range(NY):
        summed.append(
            (
                quarter(block),
                lambda t, block=block: kv_right.at[t, block],
                lambda t, block=block: kv_left.at[t, block],
                kv_sum.at[block],
            )
        )
    first = (
        lambda way: gg.at[lax.rem(z + (4, NZ - 3)[way], NZ)],
        lambda way: gu.at[lax.rem(z + (4, NZ - 3)[way], NZ)],
        lambda way: gd.at[lax.rem(z + (4, NZ - 3)[way], NZ)],
        lambda way: kv_first.at[0, way],
        lambda way: kv_first.at[1, way],
        lambda way: kv_first.at[2, way],
        lambda way: kv_first.at[3, way],
    )

    def to_right(index, step):
        buffer = summed[index][1]
        src = first[index](0) if step == 0 else buffer(step - 1)
        return remote(src, buffer(step), gr_send, gr_recv, index * 4 + step, right)

    def to_left(index, step):
        buffer = summed[index][2]
        src = first[index](1) if step == 0 else buffer(step - 1)
        return remote(src, buffer(step), gl_send, gl_recv, index * 3 + step, left)

    def ring_first(index):
        to_right(index, 0).start()
        to_left(index, 0).start()

    def ring_next(index, step):
        value, r_buffer, l_buffer, _ = summed[index]
        to_right(index, step - 1).wait_recv()
        got = r_buffer(step - 1)
        got[...] = (got[...].astype(F32) + value(lax.rem(z + 4 - step, NZ))).astype(BF)
        to_right(index, step).start()
        if step < 3:
            to_left(index, step - 1).wait_recv()
            got = l_buffer(step - 1)
            got[...] = (got[...].astype(F32) + value(lax.rem(z + NZ - 3 + step, NZ))).astype(BF)
            to_left(index, step).start()

    def ring_last(index):
        value, r_buffer, l_buffer, out = summed[index]
        to_right(index, 3).wait_recv()
        to_left(index, 2).wait_recv()
        out[...] = (
            value(z) + r_buffer(3)[...].astype(F32) + l_buffer(2)[...].astype(F32)
        ).astype(BF)

    def project():
        gather_step((0, 1, 2), 4)
        rows_in = xc[...].astype(F32)
        x = rows_in[:, :, :CAP, :].reshape(count, DS).astype(BF)
        c = rows_in[:, :, CAP:, :].reshape(count, DS).astype(BF)
        for index, (left_side, w) in enumerate(((x, wg_all), (x, wu_all), (c, wd_all))):
            product = dot(left_side, w[...].reshape(DS, FF), 1, 0)
            part[:, :, index * FF : (index + 1) * FF] = product.reshape(
                NY, NE * CAP, FF
            ).astype(BF)
        for copy in swaps():
            copy.start()

    def activate():
        for copy in swaps():
            copy.wait_recv()
        sums = part[y].astype(F32)
        for d in range(NY - 1):
            sums = sums + parts[d].astype(F32)
        gate_act = sums[:, :FF]
        up_act = sums[:, FF : 2 * FF]
        cot_down = sums[:, 2 * FF :]
        w = rows_own[:, :, D:].astype(F32)[:, :CAP, :].reshape(NE * CAP, 128)[:, :1]
        sigma = 1.0 / (1.0 + jnp.exp(-gate_act))
        silu = gate_act * sigma
        hidden = (silu * up_act).astype(BF).astype(F32)
        hidden_grad = w * cot_down
        act[y, :, :FF] = (
            hidden_grad * up_act * sigma * (1.0 + gate_act * (1.0 - sigma))
        ).astype(BF)
        act[y, :, FF : 2 * FF] = (hidden_grad * silu).astype(BF)
        act[y, :, 2 * FF :] = (w * hidden).astype(BF)
        for copy in spreads():
            copy.start()
        values = jnp.sum(hidden * cot_down, axis=1, keepdims=True)
        route[...] = jnp.broadcast_to(values, (NE * CAP, 128)).reshape(NE, CAP, 128)
        for copy in routes():
            copy.start()
        here(route.at[e], route_home.at[e], 9).start()

    def differentiate():
        for copy in spreads():
            copy.wait_recv()
        blocks = (NZ, WD, FF)
        act_all = act[...].reshape(count, 3 * FF)
        gate_pre = act_all[:, :FF]
        up_pre = act_all[:, FF : 2 * FF]
        gg[...] = dot(x_t[...], gate_pre, 1, 0).astype(BF).reshape(blocks)
        ring_first(0)
        gu[...] = dot(x_t[...], up_pre, 1, 0).astype(BF).reshape(blocks)
        ring_first(1)
        gd[...] = dot(c_t[...], act_all[:, 2 * FF :], 1, 0).astype(BF).reshape(blocks)
        ring_first(2)
        row_grad = dot(gate_pre, wg_all[...].reshape(DS, FF), 1, 1) + dot(
            up_pre, wu_all[...].reshape(DS, FF), 1, 1
        )
        row_grad = row_grad.reshape(NY, NE, CAP, DS)
        rb[...] = jnp.concatenate(
            [row_grad[:, :, :, i * 128 : (i + 1) * 128] for i in range(DS // 128)], axis=2
        ).astype(BF)
        for copy in row_swaps():
            copy.start()
        here(rb.at[y], rbuf.at[y], 10).start()

    def quarter_first(block):
        for way in range(2):
            b = lax.rem(z + (4, NZ - 3)[way], NZ)
            kv_first[block, way] = summed[3 + block][0](b).astype(BF)
        ring_first(3 + block)

    def q_home(block):
        return pltpu.make_async_remote_copy(
            src_ref=dq.at[block],
            dst_ref=dq_home.at[:, columns(y, GW)],
            send_sem=q_send.at[block],
            recv_sem=q_recv.at[y],
            device_id=(block * NZ + z, e),
            device_id_type=MESH,
        )

    def q_from(block):
        return pltpu.make_async_remote_copy(
            src_ref=dq.at[block],
            dst_ref=dq_home.at[:, block * GW : (block + 1) * GW],
            send_sem=q_send.at[block],
            recv_sem=q_recv.at[block],
            device_id=(block * NZ + z, e),
            device_id_type=MESH,
        )

    def send_q(block):
        pl.when(y != block)(lambda: q_home(block).start())

    def weights_next(step):
        for index in (0, 1, 2):
            ring_next(index, step)

    def mixed():
        differentiate()
        send_q(3)
        send_q(2)

    def second_end():
        ring_last(6)
        quarter_first(2)

    def third_end():
        ring_last(5)
        quarter_first(1)
        send_q(1)

    events = (
        (0, 0, lambda: gather_step((0, 1, 2), 2)),
        (0, 2, lambda: gather_step((0, 1, 2), 3)),
        (1, 1, project),
        (1, 2, lambda: quarter_first(3)),
        (2, 0, lambda: ring_next(6, 1)),
        (2, 2, activate),
        (3, 0, lambda: ring_next(6, 2)),
        (3, 1, lambda: ring_next(6, 3)),
        (3, 2, second_end),
        (4, 0, lambda: ring_next(5, 1)),
        (4, 2, mixed),
        (5, 0, lambda: ring_next(5, 2)),
        (5, 1, lambda: ring_next(5, 3)),
        (5, 2, third_end),
        (6, 0, lambda: weights_next(1)),
        (6, 1, lambda: ring_next(4, 1)),
        (7, 0, lambda: ring_next(4, 2)),
        (7, 1, lambda: weights_next(2)),
    )

    def work(i, carry):
        def event(sweep):
            for step, when, act_now in events:
                if when == sweep:
                    pl.when(i == step)(act_now)

        attend(NY - 1 - lax.div(i, 2), lax.rem(i, 2), event)
        return carry

    lax.fori_loop(0, STEPS, work, 0)
    quarter_first(0)
    send_q(0)
    own_q = here(dq.at[y], dq_home.at[:, columns(y, GW)], 11)
    own_q.start()

    def row_homes():
        return [
            remote(rbuf.at[:, at_e(y, z, e, d)[0]], back.at[e], i_send, i_recv, d - 1,
                   at_e(y, z, e, d)[1])
            for d in range(1, NE)
        ]

    here(rb.at[y], rbuf.at[y], 10).wait()
    for c in row_swaps():
        c.wait_recv()
    for c in row_homes():
        c.start()
    own_back = here(rbuf.at[:, e], back.at[e], 12)
    own_back.start()

    ring_next(4, 3)
    ring_next(3, 1)
    weights_next(3)
    ring_next(3, 2)
    ring_next(3, 3)
    ring_last(4)

    own_back.wait()
    for c in row_homes():
        c.wait_recv()
    pieces = back[...].astype(F32).reshape(NE, NY, DS // 128, CAP, 128)
    for block in range(NY):
        for i in range(DS // 128):
            piece = pieces[:, block, i].reshape(NE * CAP, 128).astype(BF)
            start = block * DS + i * 128
            input_grad[:, start : start + 128] = dot(dispatch[...], piece, 1, 0).astype(BF)

    def homes():
        copies = []
        for kind, out in enumerate((dk_home, dv_home)):
            target = out.at[:, columns(y, HEAD_SIZE)]
            for d in range(1, NY):
                peer, dev = at_y(y, z, e, d)
                copies.append(
                    remote(kv_sum.at[peer, kind], target, h_send, h_recv, kind * 3 + d - 1, dev)
                )
            copies.append(here(kv_sum.at[y, kind], target, 13 + kind))
        return copies

    here(route.at[e], route_home.at[e], 9).wait()
    for c in routes():
        c.wait()
    values = route_home[...].reshape(NE * CAP, 128)
    spread_values = dispatch[...].astype(F32).T * values.astype(BF).astype(F32)
    column = lax.broadcasted_iota(jnp.int32, (TOPK, TOK), 0)
    routed = jnp.zeros((TOPK, TOK), F32)
    for j in range(TOPK):
        total = jnp.sum(spread_values * named(j), axis=0, keepdims=True)
        routed += jnp.where(column == j, total, 0.0)
    route_grad[...] = routed.astype(BF)

    ring_last(3)
    for c in homes():
        c.start()
    for index in (0, 1, 2):
        ring_last(index)
    for c in homes():
        c.wait()
    for block in range(NY):
        pl.when(y != block)(lambda block=block: q_home(block).wait_send())
        pl.when(y != block)(lambda block=block: q_from(block).wait_recv())
    own_q.wait()
    for c in tokens() + kv_exchange() + q_exchange() + slices() + swaps() + spreads():
        c.wait_send()
    for c in row_swaps() + row_homes():
        c.wait_send()
    for index in range(5):
        for step in range(4):
            for c in gather(index, step):
                c.wait_send()
    for index in range(3 + NY):
        for step in range(4):
            to_right(index, step).wait_send()
            if step < 3:
                to_left(index, step).wait_send()


def layer(*arrays):
    sd = jax.ShapeDtypeStruct
    any_spec = pl.BlockSpec(memory_space=pl.ANY)
    vmem = pl.BlockSpec(memory_space=pltpu.VMEM)
    dma = pltpu.SemaphoreType.DMA
    scratch = pltpu.VMEM
    whole = (NY, NZ, TOK, HEAD_SIZE)
    length = NY * NZ * TOK
    slots = NE * CAP
    blocks = (NZ, WD, FF)
    rings = []
    pair = (2, TOK, HEAD_SIZE)
    for shape in ((NY,) + pair, (WD, FF), (WD, FF), (WD, FF)):
        rings += [scratch((4,) + shape, BF), scratch((3,) + shape, BF)]
    return pl.pallas_call(
        layer_kernel,
        out_shape=[
            sd((TOK, QUERY_HEADS * HEAD_SIZE), BF),
            sd((TOK, KEY_VALUE_HEADS * HEAD_SIZE), BF),
            sd((TOK, KEY_VALUE_HEADS * HEAD_SIZE), BF),
            sd((WD, FF), BF),
            sd((WD, FF), BF),
            sd((WD, FF), BF),
            sd((TOK, D), BF),
            sd((TOPK, TOK), BF),
        ],
        in_specs=[any_spec] * 7 + [vmem] * 4,
        out_specs=[any_spec] * 3 + [vmem] * 5,
        scratch_shapes=[
            scratch((NE, 16, D + 128), BF), scratch((TOK, slots), BF), scratch((NE, CAP, 128), F32),
            scratch((NY, TOK, GW), BF), scratch((NY, TOK, GW), BF),
            scratch(whole, BF), scratch(whole, BF), scratch((HEAD_SIZE, length), BF),
            scratch((ROWS, HEAD_SIZE), BF), scratch((ROWS, HEAD_SIZE), BF),
            scratch((length, ROWS), F32), scratch((length, ROWS), F32),
            scratch(whole, F32), scratch(whole, F32), scratch((HEAD_SIZE, ROWS), F32),
            scratch((NY, TOK, GW), BF),
            scratch((NE, 16, D + 128), BF), scratch((NY, NE, 16, DS), BF),
            scratch((DS, NY * slots), BF), scratch((DS, NY * slots), BF),
            scratch(blocks, BF), scratch(blocks, BF), scratch(blocks, BF),
            scratch((NY, slots, 3 * FF), BF), scratch((NY - 1, slots, 3 * FF), BF),
            scratch((NY, slots, 3 * FF), BF), scratch((NE, CAP, 128), F32),
            scratch((NY, NE, 32, 128), BF), scratch((NY, NE, 32, 128), BF),
            scratch((NE, NY, 32, 128), BF),
            scratch(blocks, BF), scratch(blocks, BF), scratch(blocks, BF),
        ]
        + rings
        + [
            scratch((NY, 2) + pair, BF), scratch((NY,) + pair, BF),
            dma((16,)), dma((12,)), dma((12,)), dma((7,)), dma((7,)), dma((3,)), dma((3,)),
            dma((20,)), dma((20,)), dma((15,)), dma((15,)),
            dma((3,)), dma((3,)), dma((3,)), dma((3,)), dma((7,)), dma((7,)),
            dma((4,)), dma((4,)), dma((3,)), dma((3,)), dma((7,)), dma((7,)), dma((6,)), dma((6,)),
            dma((28,)), dma((28,)), dma((21,)), dma((21,)),
        ],
        compiler_params=pltpu.CompilerParams(
            collective_id=0, has_side_effects=True, vmem_limit_bytes=VMEM_MOST
        ),
        name="layer",
    )(*arrays)


def finish_kernel(*refs):
    half = (len(refs) - 2) // 3
    held = refs[2 * half : 3 * half]
    arriving = [
        pltpu.make_async_copy(refs[i], held[i], refs[-2].at[i]) for i in range(half)
    ]
    leaving = [
        pltpu.make_async_copy(held[i], refs[half + i], refs[-1].at[i]) for i in range(half)
    ]
    for c in arriving:
        c.start()
    for first, second in zip(arriving, leaving):
        first.wait()
        second.start()
    for c in leaving:
        c.wait()


def finish(*arrays):
    any_spec = pl.BlockSpec(memory_space=pl.ANY)
    dma = pltpu.SemaphoreType.DMA
    return pl.pallas_call(
        finish_kernel,
        out_shape=[jax.ShapeDtypeStruct(a.shape, a.dtype) for a in arrays],
        in_specs=[any_spec] * len(arrays),
        out_specs=[any_spec] * len(arrays),
        scratch_shapes=[pltpu.VMEM(a.shape, a.dtype) for a in arrays]
        + [dma((len(arrays),)), dma((len(arrays),))],
        compiler_params=pltpu.CompilerParams(vmem_limit_bytes=VMEM_MOST),
        name="finish",
    )(*arrays)


def per_device(
    query_rows,
    key_matrix_all,
    value_matrix_all,
    context_grad,
    mixture_input,
    mixture_grad,
    expert_ids,
    route_weight,
    gate_weight,
    up_weight,
    down_weight,
):
    outputs = layer(
        query_rows[0], context_grad[0], key_matrix_all[0], value_matrix_all[0],
        gate_weight[0], up_weight[0], down_weight[0],
        mixture_input[0], mixture_grad[0], expert_ids[0].T, route_weight[0].T,
    )
    (
        dq_home, dk_home, dv_home, gate_grad, up_grad, down_grad, input_grad,
    ) = finish(*outputs[:7])
    route_grad = outputs[7].T
    return (
        dq_home[None],
        dk_home[None],
        dv_home[None],
        input_grad[None],
        route_grad[None],
        gate_grad[None],
        up_grad[None],
        down_grad[None],
    )


def solution(mesh):
    spec = P("exp", "ctx", None)
    return jax.shard_map(
        per_device,
        mesh=mesh,
        in_specs=(spec,) * 11,
        out_specs=(spec,) * 8,
        check_vma=False,
    )
```

profile of v0, /device:TPU:4, one launch (start us, length us, event | category | flops | bytes accessed | tf_op | source)
XLA Modules:
  0.0 152.3 jit_solution(12026685723729184568)
XLA Ops:
  0.6 147.8 %layer.1 = (bf16[128,4096]{1,0:T(8,128)(2,1)}, bf16[128,512]{1,0:T(8,128)(2,1)}, bf16[128,512]{1,0:T(8,128)(2,1)}, bf16[64,768]{1,0:T(8,128)(2,1)}, bf16[64,768]...) custom-call(bf16[128,4096]{1,0:T(8,128)(2,1)} %bitcast.25, ...), custom_call_target="tpu_custom_call" | custom-call | tf_op jit(solution)/shard_map/layer/pallas_call | solution.py:657
  148.4 2.7 %finish.1 = (bf16[128,4096]{1,0:T(8,128)(2,1)}, bf16[128,512]{1,0:T(8,128)(2,1)}, bf16[128,512]{1,0:T(8,128)(2,1)}, bf16[64,768]{1,0:T(8,128)(2,1)}, bf16[64,768...) custom-call(bf16[128,4096]{1,0:T(8,128)(2,1)} %get-tuple-element.23.refs_0_, ...), custom_call_target="tpu_custom_call" | custom-call | tf_op jit(solution)/shard_map/finish/pallas_call | solution.py:725
  151.1 0.0 copy-start
  151.1 0.7 copy-done
  151.7 0.6 copy.20
Async XLA Ops:
  151.1 0.7 copy-start
where the time goes:
time: 153 us; the launch traced here: 152 us
  Pallas kernels  150 us (98%)
    pallas_call x1, Pallas kernels, layer(): pl.pallas_call(layer_kernel, out_shape=[sd((TOK, QUERY_HEADS * HEAD_SIZE)...  148 us

commit v1 on v0

--- a/solution.py
+++ b/solution.py
@@ -225,9 +225,11 @@
     own_xc.start()
     dk_acc[...] = jnp.zeros_like(dk_acc)
     dv_acc[...] = jnp.zeros_like(dv_acc)
-    for step in range(1, 4):
-        gather_step((3, 4), step)
+    gather_step((3, 4), 1)
     gather_step((0, 1, 2), 1)
+    gather_step((3, 4), 2)
+    gather_step((3, 4), 3)
+    gather_step((0, 1, 2), 2)
     own_xc.wait()
     for c in slices():
         c.wait_recv()
@@ -509,7 +511,7 @@
             ring_next(index, step)
 
     def mixed():
-        differentiate()
+        weights_next(1)
         send_q(3)
         send_q(2)
 
@@ -523,24 +525,24 @@
         send_q(1)
 
     events = (
-        (0, 0, lambda: gather_step((0, 1, 2), 2)),
-        (0, 2, lambda: gather_step((0, 1, 2), 3)),
-        (1, 1, project),
+        (0, 0, lambda: gather_step((0, 1, 2), 3)),
+        (0, 2, project),
         (1, 2, lambda: quarter_first(3)),
         (2, 0, lambda: ring_next(6, 1)),
-        (2, 2, activate),
+        (2, 0, activate),
         (3, 0, lambda: ring_next(6, 2)),
         (3, 1, lambda: ring_next(6, 3)),
         (3, 2, second_end),
         (4, 0, lambda: ring_next(5, 1)),
+        (3, 2, differentiate),
         (4, 2, mixed),
         (5, 0, lambda: ring_next(5, 2)),
         (5, 1, lambda: ring_next(5, 3)),
         (5, 2, third_end),
-        (6, 0, lambda: weights_next(1)),
+        (6, 0, lambda: weights_next(2)),
         (6, 1, lambda: ring_next(4, 1)),
         (7, 0, lambda: ring_next(4, 2)),
-        (7, 1, lambda: weights_next(2)),
+        (7, 1, lambda: weights_next(3)),
     )
 
     def work(i, carry):
@@ -575,7 +577,6 @@
 
     ring_next(4, 3)
     ring_next(3, 1)
-    weights_next(3)
     ring_next(3, 2)
     ring_next(3, 3)
     ring_last(4)

time: 153 us -> 154 us (level)
  no operation moved by 1% of the time
where the time goes in v1:
time: 154 us; the launch traced here: 152 us
  Pallas kernels  150 us (97%)
    pallas_call x1, Pallas kernels, layer(): pl.pallas_call(layer_kernel, out_shape=[sd((TOK, QUERY_HEADS * HEAD_SIZE)...  147 us

profile of v1, /device:TPU:4, one launch (start us, length us, event | category | flops | bytes accessed | tf_op | source)
XLA Modules:
  0.0 152.1 jit_solution(6519259851078084484)
XLA Ops:
  0.6 147.5 %layer.1 = (bf16[128,4096]{1,0:T(8,128)(2,1)}, bf16[128,512]{1,0:T(8,128)(2,1)}, bf16[128,512]{1,0:T(8,128)(2,1)}, bf16[64,768]{1,0:T(8,128)(2,1)}, bf16[64,768]...) custom-call(bf16[128,4096]{1,0:T(8,128)(2,1)} %bitcast.25, ...), custom_call_target="tpu_custom_call" | custom-call | tf_op jit(solution)/shard_map/layer/pallas_call | solution.py:658
  148.1 2.7 %finish.1 = (bf16[128,4096]{1,0:T(8,128)(2,1)}, bf16[128,512]{1,0:T(8,128)(2,1)}, bf16[128,512]{1,0:T(8,128)(2,1)}, bf16[64,768]{1,0:T(8,128)(2,1)}, bf16[64,768...) custom-call(bf16[128,4096]{1,0:T(8,128)(2,1)} %get-tuple-element.23.refs_0_, ...), custom_call_target="tpu_custom_call" | custom-call | tf_op jit(solution)/shard_map/finish/pallas_call | solution.py:726
  150.8 0.0 copy-start
  150.8 0.7 copy-done
  151.5 0.6 copy.20
Async XLA Ops:
  150.8 0.7 copy-start
